TPU v7x, 256 devices: a whole 4x4x8 slice. The times are simulated.
256 devices in a mesh: section: 4 (over x_lo, core), peer: 64 (over z, y, x_hi).
Axes of the slice: x: 4 (x_hi: 2, x_lo: 2; x = x_hi * 2 + x_lo), y: 4, z: 8, core: 2. Of those that a mesh axis runs over, the one named last changes fastest.
Arguments:
- send_grads: bfloat16 [32768, 5120], P(('section', 'peer')), may hold values from -6 to 6
- wiring: int32 [32768, 1], P(('section', 'peer')), may hold values from 0 to 63; in each aligned block of 128 rows (0 to 127, 128 to 255, ...) at most 4 rows name the same one
- loss_grad: bfloat16 [16384, 5120], P('peer'), may hold values from -6 to 6
- saved_acts: bfloat16 [65536, 5120], P(('section', 'peer')), may hold values from -6 to 6
- gain: float32 [4, 5120], P('section'), may hold values from 0.1 to 1.9
- lagged_grads: bfloat16 [256, 327680], P('section', 'peer'), may hold values from -16 to 16
- weights: float32 [256, 5120], P('section'), may hold values from -6 to 6
Outputs:
- input_grads: bfloat16 [65536, 5120], P(('section', 'peer'))
- new_weights: float32 [256, 5120], P('section')
Inputs may be any that keep to these rules, and one draw needn't show every extreme that they name: `wiring`: among the rows of one device, at most 4 name the same peer; some peer is named exactly 4 times.
All inputs are finite; a program needn't handle non-finite values.
Results may differ from a plain program's by a relative error of at most 0.001.
Values may be sent and summed in bfloat16 or wider, within the bound.
A program may use at most 64 MiB of HBM per device.

v0:
```python
import jax
import jax.numpy as jnp
from jax import lax
from jax.sharding import PartitionSpec as P


def from_behind(x, axis, by):
    devices = lax.axis_size(axis)
    pairs = [(i, i + by) for i in range(devices) if 0 <= i + by < devices]
    return lax.ppermute(x, axis, pairs)


def arrange_slots(rows, wires, peers, capacity):
    dest = wires[:, 0]
    onehot = (dest[:, None] == jnp.arange(peers, dtype=jnp.int32)[None, :]).astype(jnp.int32)
    before = jnp.cumsum(onehot, axis=0) - onehot
    rank = jnp.sum(before * onehot, axis=1)
    index = dest * capacity + rank
    empty = jnp.zeros((peers * capacity, rows.shape[1]), rows.dtype)
    return empty.at[index].set(rows)


def norm_back(grads, acts, gains):
    g = grads.astype(jnp.float32)
    x = acts.astype(jnp.float32)
    scale = lax.rsqrt(jnp.mean(x * x, axis=-1, keepdims=True) + 1e-05)
    normed = x * scale
    dy = g * gains[None, :]
    inner = jnp.mean(dy * normed, axis=-1, keepdims=True)
    return (g + (dy - normed * inner) * scale).astype(jnp.bfloat16)


def per_device(send_grads, wiring, loss_grad, saved_acts, gain, lagged_grads, weights):
    rows_dev, width = send_grads.shape
    peers = lax.axis_size("peer")
    capacity = 2 * rows_dev // peers
    buffer = arrange_slots(send_grads, wiring, peers, capacity).reshape(peers, capacity, width)
    routed = lax.all_to_all(buffer, "peer", split_axis=0, concat_axis=0, tiled=True)
    moved = from_behind(routed, "section", -1)
    arrived = moved.reshape(peers * capacity, width)
    at_top = lax.axis_index("section") == lax.axis_size("section") - 1
    incoming = jnp.where(at_top, loss_grad, arrived)
    input_grads = norm_back(incoming, saved_acts, gain[0])
    summed = lax.psum(lagged_grads.astype(jnp.float32), "peer")
    new_weights = weights - 0.5 * (summed / peers)
    return (input_grads, new_weights)


def solution(mesh):
    return jax.shard_map(
        per_device,
        mesh=mesh,
        in_specs=(
            P(("section", "peer"), None),
            P(("section", "peer"), None),
            P("peer", None),
            P(("section", "peer"), None),
            P("section", None),
            P("section", "peer"),
            P("section", None),
        ),
        out_specs=(P(("section", "peer"), None), P("section", None)),
        check_vma=False,
    )
```

profile of v0, /device:TPU:2, one launch (start us, length us, event | category | flops | bytes accessed | tf_op | source)
XLA Modules:
  0.0 494.6 jit_solution(5505711904955852374)
XLA Ops:
  0.6 0.7 fusion.9
  1.4 0.2 reduce_window_sum.11
  1.5 0.8 select_reduce_fusion
  2.4 0.7 fusion.10
  3.0 4.0 scatter_custom_fusion
  7.1 2.4 reshape.23
  9.5 0.0 copy-start
  9.5 78.2 %all_to_all.5 = bf16[64,4,5120]{2,1,0:T(4,128)(2,1)} all-to-all(bf16[64,4,5120]{2,1,0:T(4,128)(2,1)} %reshape.23), channel_id=1, replica_groups=mesh['section'=4,'peer'=64] {'peer'}, dimensions={0} | all-to-all | bytes 5242880 | tf_op jit(solution)/shard_map/all_to_all | solution.py:38
  87.7 0.0 copy-start.3
  87.7 2.0 collective-permute-start
  89.8 0.0 copy-done
  89.8 0.6 fusion.6
  90.4 0.0 copy-done.3
  90.4 388.9 %all-reduce.1 = f32[64,5120]{1,0:T(8,128)} all-reduce(bf16[64,5120]{1,0:T(8,128)(2,1)S(1)} %copy-done.3), channel_id=1, replica_groups=mesh['section'=4,'peer'=64] {'peer'}, use_global_device_ids=true, to_apply=%region_5.6 | all-reduce | flops 327680 | bytes 1966080 | tf_op jit(solution)/shard_map/psum | solution.py:44
  479.3 2.9 multiply_subtract_fusion
  482.2 0.0 copy-start.4
  482.2 0.0 collective-permute-done
  482.2 5.2 %reshape.24 = bf16[256,5120]{1,0:T(8,128)(2,1)} reshape(bf16[64,4,5120]{2,1,0:T(4,128)(2,1)} %collective-permute-done) | data formatting | bytes 5242880 | tf_op jit(solution)/shard_map/reshape | solution.py:40
  487.5 0.0 copy-done.4
  487.5 0.0 copy-start.1
  487.5 3.4 fusion.3
  490.9 0.0 copy-done.1
  490.9 0.0 copy-done.2
  490.9 3.7 fusion.5
  (3 shorter events, 0.0 us)
Async XLA Ops:
  9.5 80.3 %copy-start = (bf16[256,5120]{1,0:T(8,128)(2,1)S(1)}, bf16[256,5120]{1,0:T(8,128)(2,1)}, u32[]{:S(2)}) copy-start(bf16[256,5120]{1,0:T(8,128)(2,1)} %param.10) | copy-start | bytes 7864324
  87.7 2.7 copy-start.3
  87.7 394.5 %collective-permute-start = (bf16[64,4,5120]{2,1,0:T(4,128)(2,1)}, bf16[64,4,5120]{2,1,0:T(4,128)(2,1)}, u32[]{:S(2)}, u32[]{:S(2)}) collective-permute-start(bf16[64,4,5120]{2,1,0:T(4,128)(2,1)} %all_to_all.5), channel_id=1, source_target_pairs={{64,0},{128,64},{192,128},{65,1},{129,65},{193,129},{66,2},{130,66... | collective-permute-start | bytes 7864328 | tf_op jit(solution)/shard_map/ppermute | solution.py:10
  482.2 5.2 %copy-start.4 = (f32[1,5120]{1,0:T(1,128)S(1)}, f32[1,5120]{1,0:T(1,128)}, u32[]{:S(2)}) copy-start(f32[1,5120]{1,0:T(1,128)} %param.11) | copy-start | bytes 61444
  487.5 3.4 copy-start.1
  487.5 3.4 copy-start.2
where the time goes:
time: 495 us
  blocking collectives  467 us (94%)
  other arithmetic  13 us (3%)
  local copies, waits for them, and re-layouts  11.7 us (2%)
    psum x1, blocking collectives, per_device(): summed = lax.psum(lagged_grads.astype(jnp.float32), 'peer')  389 us
    all_to_all x1, blocking collectives, per_device(): lax.all_to_all(buffer, 'peer', split_axis=0, concat_axis=0, tiled=True)  78.2 us
  transfers between devices with their start and end apart: 1, of which 0 were waited for; matrix products, arithmetic and copies ran while one was open for 1% of the time, Pallas kernels for 0%

commit v1 on v0

v1 whole, which is shorter than its diff:
```python
import functools

import jax
import jax.numpy as jnp
from jax import lax
from jax.experimental import pallas as pl
from jax.experimental.pallas import tpu as pltpu
from jax.sharding import PartitionSpec as P

MESH = pl.DeviceIdType.MESH
SLOTS = 256
CAP = 4
PIECES = 8
AHEAD = 8


def place():
    s = lax.axis_index("section")
    p = lax.axis_index("peer")
    return s, p // 8, (p // 2) % 4, p % 2


def iota(shape, dim):
    return lax.broadcasted_iota(jnp.int32, shape, dim)


def slot_matrix(wire, z, y, h):
    rows = wire.shape[1]
    r, c = iota((rows, rows), 0), iota((rows, rows), 1)
    across = jnp.broadcast_to(wire, (rows, rows))
    down = jnp.sum(jnp.where(r == c, across, 0), axis=1, keepdims=True)
    rank = jnp.sum(jnp.where((down == across) & (r < c), 1, 0), axis=0, keepdims=True)
    key = wire * CAP + rank
    i = iota((SLOTS, rows), 0)
    dh, d, dy, k = i >> 7, (i >> 4) & 7, (i >> 2) & 3, i & 3
    q = ((z + d) & 7) * 8 + ((y + dy) & 3) * 2 + ((h + dh) & 1)
    return jnp.where(q * CAP + k == key, 1.0, 0.0).astype(jnp.bfloat16)


def regroup_matrix():
    o, i = iota((SLOTS, SLOTS), 0), iota((SLOTS, SLOTS), 1)
    dy, dh, d, k = o >> 6, (o >> 5) & 1, (o >> 2) & 7, o & 3
    return jnp.where(dh * 128 + d * 16 + dy * 4 + k == i, 1.0, 0.0).astype(jnp.bfloat16)


def natural_matrix(z, y, h):
    n, o = iota((SLOTS, SLOTS), 0), iota((SLOTS, SLOTS), 1)
    zs, ys, hs, k = n >> 5, (n >> 3) & 3, (n >> 2) & 1, n & 3
    d, dy, dh = (z - zs) & 7, (y - ys) & 3, (h - hs) & 1
    return jnp.where((dy * 2 + dh) * 32 + d * 4 + k == o, 1.0, 0.0).astype(jnp.bfloat16)


def exchange(pieces, cols, wire, rows_ref, lag_ref, w_ref, arrived, new_w,
             send1, recv1, send2, slots, regroup, lag_in, part, part_in, fresh,
             s0, r0, s1, r1, s2, r2, sa, ra, local):
    s, z, y, h = place()
    width = lag_ref.shape[1]
    block = width // 8

    def at(section, dz, dy, dh):
        peer = ((z + dz) % 8) * 8 + ((y + dy) % 4) * 2 + (h + dh) % 2
        return (section, peer)

    def push(src, dst, ssem, rsem, to):
        return pltpu.make_async_remote_copy(src_ref=src, dst_ref=dst, send_sem=ssem, recv_sem=rsem,
                                            device_id=to, device_id_type=MESH)

    me = at(s, 0, 0, 0)
    barrier = pltpu.get_barrier_semaphore()
    for d in range(1, 8):
        pl.semaphore_signal(barrier, inc=1, device_id=at(s, d, 0, 0), device_id_type=MESH)
    for e in range(8):
        for ds in range(4):
            if e or ds:
                pl.semaphore_signal(barrier, inc=1, device_id=at((s + ds) % 4, 0, e // 2, e % 2), device_id_type=MESH)

    sends = s >= 1
    crossing = lambda i: lax.rem(i, 2) == 1

    slots[...] = slot_matrix(wire[...], z, y, h)
    regroup[...] = regroup_matrix()

    def span(i):
        return pl.ds(pl.multiple_of(i * cols, 128), cols)

    def arrange(i, carry):
        out = jnp.dot(slots[...], rows_ref[:, span(i)], preferred_element_type=jnp.float32).astype(jnp.bfloat16)
        out = out.reshape(2, 128, cols)
        send1[i] = out
        recv1[i, :, 0:16, :] = out[:, 0:16, :]
        return carry

    @pl.when((s == 1) | (s == 3))
    def _():
        lax.fori_loop(0, pieces, arrange, 0)

    @pl.when(s == 2)
    def _():
        lax.fori_loop(0, pieces, arrange, 0)

    pl.semaphore_wait(barrier, 38)

    def lag_copy(e):
        dy, dh = e // 2, e % 2
        j = ((y + dy) % 4) * 2 + (h + dh) % 2
        return push(lag_ref.at[:, pl.ds(pl.multiple_of(j * block, 128), block)], lag_in.at[e - 1], sa.at[0], ra.at[0],
                    at(s, 0, dy, dh))

    for e in range(1, 8):
        lag_copy(e).start()

    def along_z(i, d):
        lines = pl.ds(d * 16, 16)
        return push(send1.at[i, :, lines, :], recv1.at[i, :, lines, :], s1.at[i], r1.at[i], at(s, d, 0, 0))

    def along_z_all(i):
        lines = pl.ds(16, 112)
        return push(send1.at[i, :, lines, :], recv1.at[i, :, lines, :], s1.at[i], r1.at[i], at(s, 1, 0, 0))

    def start_z(i):
        for d in (4, 3, 5, 2, 6, 1, 7):
            along_z(i, d).start()

    def cross(i, dh, first):
        lines = pl.ds(0, 16) if first else pl.ds(16, 112)
        return push(send1.at[i, dh, lines, :], (recv1 if first else send1).at[i, dh, lines, :],
                    s0.at[i], r0.at[i], at(0, 0, 0, dh))

    def whole(buffer, i, ssem, rsem):
        return push(buffer.at[i], buffer.at[i], ssem.at[i], rsem.at[i], at((s + 3) % 4, 0, 0, 0))

    def start_out(i, carry):
        @pl.when((s == 1) | (s == 3) | ((s == 2) & ~crossing(i)))
        def _():
            start_z(i)

        @pl.when((s == 2) & crossing(i))
        def _():
            for dh in range(2):
                cross(i, dh, False).start()
                cross(i, dh, True).start()

        return carry

    lax.fori_loop(0, pieces, start_out, 0)

    @pl.when(s == 0)
    def _():
        def onward(i, carry):
            @pl.when(crossing(i))
            def _():
                whole(send2, i, s0, r0).wait_recv()
                start_z(i)
            return carry
        lax.fori_loop(0, pieces, onward, 0)

    mine = (y * 2 + h) * block
    own = pl.ds(pl.multiple_of(mine, 128), block)
    zrows = pl.ds(pl.multiple_of(z * 8, 8), 8)

    def lag_sum():
        push(lag_in, lag_in, sa.at[0], ra.at[0], me).wait_recv()
        total = lag_ref[:, own].astype(jnp.float32)
        for e in range(7):
            total = total + lag_in[e].astype(jnp.float32)
        part[...] = total
        for d in range(1, 8):
            to = (z + d) % 8
            push(part.at[pl.ds(pl.multiple_of(to * 8, 8), 8)], part_in.at[d - 1], sa.at[1], ra.at[1],
                 at(s, d, 0, 0)).start()

    def update():
        push(part_in, part_in, sa.at[1], ra.at[1], me).wait_recv()
        total = part[zrows, :]
        for d in range(7):
            total = total + part_in[d]
        fresh[...] = w_ref[zrows, own] - 0.5 * (total / 64.0)
        for d in range(1, 8):
            push(fresh, new_w.at[zrows, own], sa.at[2], ra.at[2], at(s, d, 0, 0)).start()
        pltpu.make_async_copy(fresh, new_w.at[zrows, own], local).start()

    def gather_h():
        push(part_in, part_in, sa.at[2], ra.at[2], me).wait_recv()
        pltpu.make_async_copy(fresh, new_w.at[zrows, own], local).wait()
        push(new_w.at[:, own], new_w.at[:, own], sa.at[3], ra.at[3], at(s, 0, 0, 1)).start()

    pair = pl.ds(pl.multiple_of(y * 2 * block, 128), 2 * block)

    def gather_y():
        push(part, part, sa.at[3], ra.at[3], me).wait_recv()
        for dy in (2, 1, 3):
            push(new_w.at[:, pair], new_w.at[:, pair], sa.at[4], ra.at[4], at(s, 0, dy, 0)).start()

    three = pl.ds(0, 6 * block)

    def relay(i):
        along_z_all(i).wait_recv()
        data = recv1[i].reshape(SLOTS, cols)
        send2[i] = jnp.dot(regroup[...], data, preferred_element_type=jnp.float32).astype(jnp.bfloat16)

        @pl.when(s >= 1)
        def _():
            for e in (4, 5, 2, 3, 6, 7, 1, 0):
                lines = pl.ds(e * 32, 32)
                push(send2.at[i, lines, :], arrived.at[i, lines, :], s2.at[i], r2.at[i],
                     at((s + 3) % 4, 0, e // 2, e % 2)).start()

        @pl.when(s == 0)
        def _():
            for dy in (2, 1, 3, 0):
                lines = pl.ds(dy * 64, 64)
                push(send2.at[i, lines, :], arrived.at[i, lines, :], s2.at[i], r2.at[i], at(1, 0, dy, 0)).start()

    relays = lambda i: (s == 1) | (s == 3) | ((s == 2) & ~crossing(i)) | ((s == 0) & crossing(i))

    def step(i, carry):
        pl.when(i == 0)(lag_sum)
        pl.when(i == 1)(update)
        pl.when(i == 2)(gather_h)
        pl.when(i == 3)(gather_y)
        pl.when(relays(i))(lambda: relay(i))
        return carry

    lax.fori_loop(0, pieces, step, 0)

    def finish(i, carry):
        @pl.when(relays(i))
        def _():
            along_z_all(i).wait_send()
            whole(send2, i, s2, r2).wait_send()

        @pl.when((s == 2) & crossing(i))
        def _():
            whole(send2, i, s0, r0).wait_send()

        @pl.when(s <= 2)
        def _():
            whole(arrived, i, s2, r2).wait_recv()

        return carry

    lax.fori_loop(0, pieces, finish, 0)
    push(lag_in, lag_in, sa.at[0], ra.at[0], me).wait_send()
    push(part_in, part_in, sa.at[1], ra.at[1], me).wait_send()
    push(part_in, part_in, sa.at[2], ra.at[2], me).wait_send()
    push(part, part, sa.at[3], ra.at[3], me).wait_send()
    push(new_w.at[:, three], new_w.at[:, three], sa.at[4], ra.at[4], me).wait()


def norm(pieces, cols, arrived, loss, acts, gain, out, grads, natural):
    s, z, y, h = place()
    width = acts.shape[1]
    natural[...] = natural_matrix(z, y, h)

    def span(i):
        return pl.ds(pl.multiple_of(i * cols, 128), cols)

    @pl.when(s == 3)
    def _():
        grads[...] = loss[...]

    def bring(i, carry):
        @pl.when(s < 3)
        def _():
            grads[:, span(i)] = jnp.dot(natural[...], arrived[i], preferred_element_type=jnp.float32).astype(jnp.bfloat16)
        return carry

    lax.fori_loop(0, pieces, bring, 0)

    def lines(b, carry):
        rows = pl.ds(pl.multiple_of(b * 16, 16), 16)

        def sums(i, both):
            x = acts[rows, span(i)].astype(jnp.float32)
            g = grads[rows, span(i)].astype(jnp.float32)
            a = jnp.sum(x * x, axis=1, keepdims=True)
            c = jnp.sum(g * gain[:, span(i)] * x, axis=1, keepdims=True)
            return both[0] + a, both[1] + c

        zero = jnp.zeros((16, 1), jnp.float32)
        a, c = lax.fori_loop(0, pieces, sums, (zero, zero), unroll=True)
        r = lax.rsqrt(a / width + 1e-05)
        inner = c * r / width

        def last(i, carry):
            x = acts[rows, span(i)].astype(jnp.float32)
            g = grads[rows, span(i)].astype(jnp.float32)
            out[rows, span(i)] = (g + (g * gain[:, span(i)] - (x * r) * inner) * r).astype(jnp.bfloat16)
            return carry

        lax.fori_loop(0, pieces, last, 0, unroll=True)
        return carry

    lax.fori_loop(0, SLOTS // 16, lines, 0)


def per_device(send_grads, wiring, loss_grad, saved_acts, gain, lagged_grads, weights):
    rows, width = send_grads.shape
    pieces, cols = PIECES, width // PIECES
    depth = lagged_grads.shape[0]
    block = width // 8
    vmem = pl.BlockSpec(memory_space=pltpu.VMEM)
    hbm = pl.BlockSpec(memory_space=pl.ANY)
    bf16, f32 = jnp.bfloat16, jnp.float32
    dma = pltpu.SemaphoreType.DMA
    arrived, new_weights = pl.pallas_call(
        functools.partial(exchange, pieces, cols),
        out_shape=(
            jax.ShapeDtypeStruct((pieces, SLOTS, cols), bf16),
            jax.ShapeDtypeStruct((depth, width), f32),
        ),
        in_specs=[vmem] * 4,
        out_specs=(hbm, hbm),
        scratch_shapes=[
            pltpu.VMEM((pieces, 2, 128, cols), bf16),
            pltpu.VMEM((pieces, 2, 128, cols), bf16),
            pltpu.VMEM((pieces, SLOTS, cols), bf16),
            pltpu.VMEM((SLOTS, rows), bf16),
            pltpu.VMEM((SLOTS, SLOTS), bf16),
            pltpu.VMEM((7, depth, block), bf16),
            pltpu.VMEM((depth, block), f32),
            pltpu.VMEM((7, 8, block), f32),
            pltpu.VMEM((8, block), f32),
            dma((pieces,)), dma((pieces,)), dma((pieces,)), dma((pieces,)), dma((pieces,)), dma((pieces,)),
            dma((5,)), dma((5,)), dma(()),
        ],
        compiler_params=pltpu.CompilerParams(
            collective_id=0, has_side_effects=True, vmem_limit_bytes=48 * 1024 * 1024
        ),
        name="exchange",
    )(wiring.reshape(1, rows), send_grads, lagged_grads, weights)
    input_grads = pl.pallas_call(
        functools.partial(norm, pieces, cols),
        out_shape=jax.ShapeDtypeStruct((SLOTS, width), bf16),
        in_specs=[vmem] * 4,
        out_specs=vmem,
        scratch_shapes=[
            pltpu.VMEM((SLOTS, width), bf16),
            pltpu.VMEM((SLOTS, SLOTS), bf16),
        ],
        compiler_params=pltpu.CompilerParams(vmem_limit_bytes=48 * 1024 * 1024),
        name="norm",
    )(arrived, loss_grad, saved_acts, gain)
    return (input_grads, new_weights)


def solution(mesh):
    return jax.shard_map(
        per_device,
        mesh=mesh,
        in_specs=(
            P(("section", "peer"), None),
            P(("section", "peer"), None),
            P("peer", None),
            P(("section", "peer"), None),
            P("section", None),
            P("section", "peer"),
            P("section", None),
        ),
        out_specs=(P(("section", "peer"), None), P("section", None)),
        check_vma=False,
    )
```

time: 495 us -> 119 us (0.24)
  the two profiles are of different devices: /device:TPU:2 before, /device:TPU:1 now
where the time goes in v1:
time: 119 us
  Pallas kernels  111 us (93%)
  local copies, waits for them, and re-layouts  7.31 us (6%)
    pallas_call x1, Pallas kernels, per_device(): pl.pallas_call(functools.partial(exchange, pieces, cols), out_shape=(jax....  102 us
    pallas_call x1, Pallas kernels, per_device(): pl.pallas_call(functools.partial(norm, pieces, cols), out_shape=jax.Shape...  8.95 us
    unnamed x15, local copies, waits for them, and re-layouts  7.31 us

profile of v1, /device:TPU:1, one launch (start us, length us, event | category | flops | bytes accessed | tf_op | source)
XLA Modules:
  0.0 119.1 jit_solution(12390807652190885856)
XLA Ops:
  0.6 0.0 copy-start
  0.6 0.0 copy-start.2
  0.7 1.5 %copy-done.2 = bf16[128,5120]{1,0:T(8,128)(2,1)S(1)} copy-done((bf16[128,5120]{1,0:T(8,128)(2,1)S(1)}, bf16[128,5120]{1,0:T(8,128)(2,1)}, u32[]{:S(2)}) %copy-start.2) | copy-done | bytes 1310744
  2.1 0.0 copy-start.3
  2.1 1.3 %copy-done.3 = f32[64,5120]{1,0:T(8,128)S(1)} copy-done((f32[64,5120]{1,0:T(8,128)S(1)}, f32[64,5120]{1,0:T(8,128)}, u32[]{:S(2)}) %copy-start.3) | copy-done | bytes 1310744
  3.4 0.0 copy-start.4
  3.4 1.1 copy-done.4
  4.5 0.0 copy-start.6
  4.5 0.7 copy-done.6
  5.2 0.0 copy-start.5
  5.2 102.2 %exchange.1 = (bf16[8,256,640]{2,1,0:T(8,128)(2,1)}, f32[64,5120]{1,0:T(8,128)S(1)}) custom-call(s32[1,128]{1,0:T(1,128)S(1)} %bitcast.1, bf16[128,5120]{1,0:T(8,128)(2,1)S(1)} %copy-done.2, bf16[64,5120]{1,0:T(8,128)(2,1)S(1)} %copy-done.4, f32[64,5120]{1,0:T(8,128)S(1)} %copy-done.3), custom_call_target="tpu_custom_call" | custom-call | tf_op jit(solution)/shard_map/exchange/pallas_call | solution.py:306
  107.4 0.0 copy-done
  107.4 0.0 copy-done.5
  107.4 0.0 copy-start.1
  107.4 1.7 %copy-done.1 = bf16[8,256,640]{2,1,0:T(8,128)(2,1)S(1)} copy-done((bf16[8,256,640]{2,1,0:T(8,128)(2,1)S(1)}, bf16[8,256,640]{2,1,0:T(8,128)(2,1)}, u32[]{:S(2)}) %copy-start.1) | copy-done | bytes 2621464
  109.1 9.0 %norm.1 = bf16[256,5120]{1,0:T(8,128)(2,1)} custom-call(bf16[8,256,640]{2,1,0:T(8,128)(2,1)S(1)} %copy-done.1, bf16[256,5120]{1,0:T(8,128)(2,1)S(1)} %copy-done, bf16[256,5120]{1,0:T(8,128)(2,1)} %acts.1, f32[1,5120]{1,0:T(1,128)S(1)} %copy-done.5), custom_call_target="tpu_custom_call" | custom-call | tf_op jit(solution)/shard_map/norm/pallas_call | solution.py:332
  118.1 1.1 copy.10
Async XLA Ops:
  0.6 106.7 %copy-start = (bf16[256,5120]{1,0:T(8,128)(2,1)S(1)}, bf16[256,5120]{1,0:T(8,128)(2,1)}, u32[]{:S(2)}) copy-start(bf16[256,5120]{1,0:T(8,128)(2,1)} %loss.1) | copy-start | bytes 7864324
  0.6 1.5 %copy-start.2 = (bf16[128,5120]{1,0:T(8,128)(2,1)S(1)}, bf16[128,5120]{1,0:T(8,128)(2,1)}, u32[]{:S(2)}) copy-start(bf16[128,5120]{1,0:T(8,128)(2,1)} %rows_ref.1) | copy-start | bytes 3932164
  2.1 1.3 %copy-start.3 = (f32[64,5120]{1,0:T(8,128)S(1)}, f32[64,5120]{1,0:T(8,128)}, u32[]{:S(2)}) copy-start(f32[64,5120]{1,0:T(8,128)} %w_ref.1) | copy-start | bytes 3932164
  3.4 1.1 copy-start.4
  4.5 0.7 copy-start.6
  5.2 102.2 %copy-start.5 = (f32[1,5120]{1,0:T(1,128)S(1)}, f32[1,5120]{1,0:T(1,128)}, u32[]{:S(2)}) copy-start(f32[1,5120]{1,0:T(1,128)} %gain.1) | copy-start | bytes 61444
  107.4 1.7 %copy-start.1 = (bf16[8,256,640]{2,1,0:T(8,128)(2,1)S(1)}, bf16[8,256,640]{2,1,0:T(8,128)(2,1)}, u32[]{:S(2)}) copy-start(bf16[8,256,640]{2,1,0:T(8,128)(2,1)} %get-tuple-element.4.arrived) | copy-start | bytes 7864324

commit v2 on v1

--- a/solution.py
+++ b/solution.py
@@ -10,8 +10,9 @@
 MESH = pl.DeviceIdType.MESH
 SLOTS = 256
 CAP = 4
-PIECES = 8
-AHEAD = 8
+PIECES = 10
+AHEAD = 3
+LAG = 4
 
 
 def place():
@@ -50,12 +51,15 @@
     return jnp.where((dy * 2 + dh) * 32 + d * 4 + k == o, 1.0, 0.0).astype(jnp.bfloat16)
 
 
-def exchange(pieces, cols, wire, rows_ref, lag_ref, w_ref, arrived, new_w,
-             send1, recv1, send2, slots, regroup, lag_in, part, part_in, fresh,
-             s0, r0, s1, r1, s2, r2, sa, ra, local):
+def exchange(pieces, cols, wire, gain, rows_hbm, lag_ref, w_ref, loss, acts_hbm, out_hbm, new_w,
+             send1, recv1, send2, arrived, rows_ref, acts, grads, out, squares, products,
+             slots, regroup, natural, lag_own, lag_in, part, part_in, fresh, w_own,
+             s0, r0, s1, r1, s2, r2, sa, ra, local, row_sem, out_sem):
     s, z, y, h = place()
     width = lag_ref.shape[1]
     block = width // 8
+    own = pl.ds(pl.multiple_of((y * 2 + h) * block, 128), block)
+    zrows = pl.ds(pl.multiple_of(z * 8, 8), 8)
 
     def at(section, dz, dy, dh):
         peer = ((z + dz) % 8) * 8 + ((y + dy) % 4) * 2 + (h + dh) % 2
@@ -74,30 +78,41 @@
             if e or ds:
                 pl.semaphore_signal(barrier, inc=1, device_id=at((s + ds) % 4, 0, e // 2, e % 2), device_id_type=MESH)
 
-    sends = s >= 1
     crossing = lambda i: lax.rem(i, 2) == 1
-
-    slots[...] = slot_matrix(wire[...], z, y, h)
-    regroup[...] = regroup_matrix()
 
     def span(i):
         return pl.ds(pl.multiple_of(i * cols, 128), cols)
 
-    def arrange(i, carry):
-        out = jnp.dot(slots[...], rows_ref[:, span(i)], preferred_element_type=jnp.float32).astype(jnp.bfloat16)
-        out = out.reshape(2, 128, cols)
-        send1[i] = out
-        recv1[i, :, 0:16, :] = out[:, 0:16, :]
-        return carry
-
-    @pl.when((s == 1) | (s == 3))
+    def fetch(i):
+        return pltpu.make_async_copy(rows_hbm.at[:, span(i)], rows_ref.at[:, span(i)], row_sem.at[i])
+
+    fetch_lag = pltpu.make_async_copy(lag_ref.at[:, own], lag_own, local.at[1])
+    fetch_w = pltpu.make_async_copy(w_ref.at[zrows, own], w_own, local.at[2])
+    fetch_acts = pltpu.make_async_copy(acts_hbm, acts, local.at[3])
+    fetch_loss = pltpu.make_async_copy(loss, grads, local.at[4])
+
+    @pl.when(s >= 1)
     def _():
-        lax.fori_loop(0, pieces, arrange, 0)
-
-    @pl.when(s == 2)
-    def _():
-        lax.fori_loop(0, pieces, arrange, 0)
-
+        for i in range(pieces):
+            fetch(i).start()
+
+    fetch_lag.start()
+    fetch_w.start()
+    fetch_acts.start()
+    pl.when(s == 3)(fetch_loss.start)
+    squares[...] = jnp.zeros_like(squares)
+    products[...] = jnp.zeros_like(products)
+
+    slots[...] = slot_matrix(wire[...], z, y, h)
+
+    def arrange(i):
+        fetch(i).wait()
+        data = jnp.dot(slots[...], rows_ref[:, span(i)], preferred_element_type=jnp.float32).astype(jnp.bfloat16)
+        data = data.reshape(2, 128, cols)
+        send1[i] = data
+        recv1[i, :, 0:16, :] = data[:, 0:16, :]
+
+    pl.when(s >= 1)(lambda: arrange(0))
     pl.semaphore_wait(barrier, 38)
 
     def lag_copy(e):
@@ -142,25 +157,33 @@
 
         return carry
 
-    lax.fori_loop(0, pieces, start_out, 0)
+    start_out(0, 0)
+
+    @pl.when(s >= 1)
+    def _():
+        def arrange_start(i, carry):
+            arrange(i)
+            pl.when(i < AHEAD)(lambda: (start_out(i, 0), None)[1])
+            return carry
+        lax.fori_loop(1, pieces, arrange_start, 0)
+
+    regroup[...] = regroup_matrix()
+    natural[...] = natural_matrix(z, y, h)
+    fetch_acts.wait()
+    pl.when(s == 3)(fetch_loss.wait)
+
+    def onward(i):
+        whole(send2, i, s0, r0).wait_recv()
+        start_z(i)
 
     @pl.when(s == 0)
     def _():
-        def onward(i, carry):
-            @pl.when(crossing(i))
-            def _():
-                whole(send2, i, s0, r0).wait_recv()
-                start_z(i)
-            return carry
-        lax.fori_loop(0, pieces, onward, 0)
-
-    mine = (y * 2 + h) * block
-    own = pl.ds(pl.multiple_of(mine, 128), block)
-    zrows = pl.ds(pl.multiple_of(z * 8, 8), 8)
+        onward(1)
 
     def lag_sum():
         push(lag_in, lag_in, sa.at[0], ra.at[0], me).wait_recv()
-        total = lag_ref[:, own].astype(jnp.float32)
+        fetch_lag.wait()
+        total = lag_own[...].astype(jnp.float32)
         for e in range(7):
             total = total + lag_in[e].astype(jnp.float32)
         part[...] = total
@@ -174,14 +197,15 @@
         total = part[zrows, :]
         for d in range(7):
             total = total + part_in[d]
-        fresh[...] = w_ref[zrows, own] - 0.5 * (total / 64.0)
+        fetch_w.wait()
+        fresh[...] = w_own[...] - 0.5 * (total / 64.0)
         for d in range(1, 8):
             push(fresh, new_w.at[zrows, own], sa.at[2], ra.at[2], at(s, d, 0, 0)).start()
-        pltpu.make_async_copy(fresh, new_w.at[zrows, own], local).start()
+        pltpu.make_async_copy(fresh, new_w.at[zrows, own], local.at[0]).start()
 
     def gather_h():
         push(part_in, part_in, sa.at[2], ra.at[2], me).wait_recv()
-        pltpu.make_async_copy(fresh, new_w.at[zrows, own], local).wait()
+        pltpu.make_async_copy(fresh, new_w.at[zrows, own], local.at[0]).wait()
         push(new_w.at[:, own], new_w.at[:, own], sa.at[3], ra.at[3], at(s, 0, 0, 1)).start()
 
     pair = pl.ds(pl.multiple_of(y * 2 * block, 128), 2 * block)
@@ -194,7 +218,6 @@
     three = pl.ds(0, 6 * block)
 
     def relay(i):
-        along_z_all(i).wait_recv()
         data = recv1[i].reshape(SLOTS, cols)
         send2[i] = jnp.dot(regroup[...], data, preferred_element_type=jnp.float32).astype(jnp.bfloat16)
 
@@ -211,17 +234,67 @@
                 lines = pl.ds(dy * 64, 64)
                 push(send2.at[i, lines, :], arrived.at[i, lines, :], s2.at[i], r2.at[i], at(1, 0, dy, 0)).start()
 
+    def squared(i):
+        x = acts[:, span(i)].astype(jnp.float32)
+        products_x = x * x
+        total = squares[...]
+        for c in range(cols // 128):
+            total = total + products_x[:, c * 128:(c + 1) * 128]
+        squares[...] = total
+
+    def multiplied(i, g):
+        terms = g * gain[:, span(i)] * acts[:, span(i)].astype(jnp.float32)
+        total = products[...]
+        for c in range(cols // 128):
+            total = total + terms[:, c * 128:(c + 1) * 128]
+        products[...] = total
+
+    def take(i):
+        whole(arrived, i, s2, r2).wait_recv()
+        g = jnp.dot(natural[...], arrived[i], preferred_element_type=jnp.float32)
+        grads[:, span(i)] = g.astype(jnp.bfloat16)
+        multiplied(i, g)
+
     relays = lambda i: (s == 1) | (s == 3) | ((s == 2) & ~crossing(i)) | ((s == 0) & crossing(i))
 
     def step(i, carry):
-        pl.when(i == 0)(lag_sum)
-        pl.when(i == 1)(update)
-        pl.when(i == 2)(gather_h)
-        pl.when(i == 3)(gather_y)
+        pl.when(i == 1)(lag_sum)
+        pl.when(i == 3)(update)
+        pl.when(i == 5)(gather_h)
+        pl.when(i == 6)(gather_y)
+        pl.when(relays(i))(lambda: along_z_all(i).wait_recv())
+        pl.when((s == 0) & ~crossing(i) & (i + 3 < pieces))(lambda: onward(i + 3))
+        pl.when(i + AHEAD < pieces)(lambda: (start_out(i + AHEAD, 0), None)[1])
         pl.when(relays(i))(lambda: relay(i))
+        squared(i)
+        pl.when(s == 3)(lambda: multiplied(i, grads[:, span(i)].astype(jnp.float32)))
+        pl.when((s < 3) & (i >= LAG))(lambda: take(i - LAG))
         return carry
 
     lax.fori_loop(0, pieces, step, 0)
+
+    @pl.when(s < 3)
+    def _():
+        lax.fori_loop(pieces - LAG, pieces, lambda i, carry: (take(i), carry)[1], 0)
+
+    def emit(b):
+        rows = pl.ds(pl.multiple_of(b * 32, 32), 32)
+        return pltpu.make_async_copy(out.at[rows, :], out_hbm.at[rows, :], out_sem.at[b])
+
+    def last(b, carry):
+        for part_of in range(2):
+            rows = pl.ds(pl.multiple_of(b * 32 + part_of * 16, 16), 16)
+            r = lax.rsqrt(jnp.sum(squares[rows, :], axis=1, keepdims=True) / width + 1e-05)
+            inner = jnp.sum(products[rows, :], axis=1, keepdims=True) * r / width
+            for c in range(pieces):
+                at_cols = slice(c * cols, (c + 1) * cols)
+                x = acts[rows, at_cols].astype(jnp.float32)
+                g = grads[rows, at_cols].astype(jnp.float32)
+                out[rows, at_cols] = (g + (g * gain[:, at_cols] - (x * r) * inner) * r).astype(jnp.bfloat16)
+        emit(b).start()
+        return carry
+
+    lax.fori_loop(0, SLOTS // 32, last, 0)
 
     def finish(i, carry):
         @pl.when(relays(i))
@@ -232,10 +305,6 @@
         @pl.when((s == 2) & crossing(i))
         def _():
             whole(send2, i, s0, r0).wait_send()
-
-        @pl.when(s <= 2)
-        def _():
-            whole(arrived, i, s2, r2).wait_recv()
 
         return carry
 
@@ -245,53 +314,7 @@
     push(part_in, part_in, sa.at[2], ra.at[2], me).wait_send()
     push(part, part, sa.at[3], ra.at[3], me).wait_send()
     push(new_w.at[:, three], new_w.at[:, three], sa.at[4], ra.at[4], me).wait()
-
-
-def norm(pieces, cols, arrived, loss, acts, gain, out, grads, natural):
-    s, z, y, h = place()
-    width = acts.shape[1]
-    natural[...] = natural_matrix(z, y, h)
-
-    def span(i):
-        return pl.ds(pl.multiple_of(i * cols, 128), cols)
-
-    @pl.when(s == 3)
-    def _():
-        grads[...] = loss[...]
-
-    def bring(i, carry):
-        @pl.when(s < 3)
-        def _():
-            grads[:, span(i)] = jnp.dot(natural[...], arrived[i], preferred_element_type=jnp.float32).astype(jnp.bfloat16)
-        return carry
-
-    lax.fori_loop(0, pieces, bring, 0)
-
-    def lines(b, carry):
-        rows = pl.ds(pl.multiple_of(b * 16, 16), 16)
-
-        def sums(i, both):
-            x = acts[rows, span(i)].astype(jnp.float32)
-            g = grads[rows, span(i)].astype(jnp.float32)
-            a = jnp.sum(x * x, axis=1, keepdims=True)
-            c = jnp.sum(g * gain[:, span(i)] * x, axis=1, keepdims=True)
-            return both[0] + a, both[1] + c
-
-        zero = jnp.zeros((16, 1), jnp.float32)
-        a, c = lax.fori_loop(0, pieces, sums, (zero, zero), unroll=True)
-        r = lax.rsqrt(a / width + 1e-05)
-        inner = c * r / width
-
-        def last(i, carry):
-            x = acts[rows, span(i)].astype(jnp.float32)
-            g = grads[rows, span(i)].astype(jnp.float32)
-            out[rows, span(i)] = (g + (g * gain[:, span(i)] - (x * r) * inner) * r).astype(jnp.bfloat16)
-            return carry
-
-        lax.fori_loop(0, pieces, last, 0, unroll=True)
-        return carry
-
-    lax.fori_loop(0, SLOTS // 16, lines, 0)
+    lax.fori_loop(0, SLOTS // 32, lambda b, carry: (emit(b).wait(), carry)[1], 0)
 
 
 def per_device(send_grads, wiring, loss_grad, saved_acts, gain, lagged_grads, weights):
@@ -303,45 +326,42 @@
     hbm = pl.BlockSpec(memory_space=pl.ANY)
     bf16, f32 = jnp.bfloat16, jnp.float32
     dma = pltpu.SemaphoreType.DMA
-    arrived, new_weights = pl.pallas_call(
+    return pl.pallas_call(
         functools.partial(exchange, pieces, cols),
         out_shape=(
-            jax.ShapeDtypeStruct((pieces, SLOTS, cols), bf16),
+            jax.ShapeDtypeStruct((SLOTS, width), bf16),
             jax.ShapeDtypeStruct((depth, width), f32),
         ),
-        in_specs=[vmem] * 4,
+        in_specs=[vmem] * 2 + [hbm] * 5,
         out_specs=(hbm, hbm),
         scratch_shapes=[
             pltpu.VMEM((pieces, 2, 128, cols), bf16),
             pltpu.VMEM((pieces, 2, 128, cols), bf16),
             pltpu.VMEM((pieces, SLOTS, cols), bf16),
+            pltpu.VMEM((pieces, SLOTS, cols), bf16),
+            pltpu.VMEM((rows, width), bf16),
+            pltpu.VMEM((SLOTS, width), bf16),
+            pltpu.VMEM((SLOTS, width), bf16),
+            pltpu.VMEM((SLOTS, width), bf16),
+            pltpu.VMEM((SLOTS, 128), f32),
+            pltpu.VMEM((SLOTS, 128), f32),
             pltpu.VMEM((SLOTS, rows), bf16),
             pltpu.VMEM((SLOTS, SLOTS), bf16),
+            pltpu.VMEM((SLOTS, SLOTS), bf16),
+            pltpu.VMEM((depth, block), bf16),
             pltpu.VMEM((7, depth, block), bf16),
             pltpu.VMEM((depth, block), f32),
             pltpu.VMEM((7, 8, block), f32),
             pltpu.VMEM((8, block), f32),
+            pltpu.VMEM((8, block), f32),
             dma((pieces,)), dma((pieces,)), dma((pieces,)), dma((pieces,)), dma((pieces,)), dma((pieces,)),
-            dma((5,)), dma((5,)), dma(()),
+            dma((5,)), dma((5,)), dma((5,)), dma((pieces,)), dma((SLOTS // 32,)),
         ],
         compiler_params=pltpu.CompilerParams(
-            collective_id=0, has_side_effects=True, vmem_limit_bytes=48 * 1024 * 1024
+            collective_id=0, has_side_effects=True, vmem_limit_bytes=60 * 1024 * 1024
         ),
         name="exchange",
-    )(wiring.reshape(1, rows), send_grads, lagged_grads, weights)
-    input_grads = pl.pallas_call(
-        functools.partial(norm, pieces, cols),
-        out_shape=jax.ShapeDtypeStruct((SLOTS, width), bf16),
-        in_specs=[vmem] * 4,
-        out_specs=vmem,
-        scratch_shapes=[
-            pltpu.VMEM((SLOTS, width), bf16),
-            pltpu.VMEM((SLOTS, SLOTS), bf16),
-        ],
-        compiler_params=pltpu.CompilerParams(vmem_limit_bytes=48 * 1024 * 1024),
-        name="norm",
-    )(arrived, loss_grad, saved_acts, gain)
-    return (input_grads, new_weights)
+    )(wiring.reshape(1, rows), gain, send_grads, lagged_grads, weights, loss_grad, saved_acts)
 
 
 def solution(mesh):

time: 119 us -> 84.9 us (0.71)
  Pallas kernels: 111 us -> 79.5 us
  local copies, waits for them, and re-layouts: 7.31 us -> 4.56 us
    pallas_call x1, Pallas kernels: 102 us -> 79.5 us  [per_device(): pl.pallas_call(functools.partial(exchange, pieces, cols), out_shape=(jax....]
    pallas_call x1 -> x0, Pallas kernels: 8.95 us -> none  [per_device(): pl.pallas_call(functools.partial(norm, pieces, cols), out_shape=jax.Shape...]
    unnamed x15 -> x4, local copies, waits for them, and re-layouts: 7.31 us -> 4.56 us
where the time goes in v2:
time: 84.9 us; the launch traced here: 84.7 us
  Pallas kernels  79.5 us (94%)
  local copies, waits for them, and re-layouts  4.56 us (5%)
    pallas_call x1, Pallas kernels, per_device(): pl.pallas_call(functools.partial(exchange, pieces, cols), out_shape=(jax....  79.5 us
    unnamed x4, local copies, waits for them, and re-layouts  4.56 us

profile of v2, /device:TPU:1, one launch (start us, length us, event | category | flops | bytes accessed | tf_op | source)
XLA Modules:
  0.0 84.7 jit_solution(10863342192301838095)
XLA Ops:
  0.6 79.5 %exchange.1 = (bf16[256,5120]{1,0:T(8,128)(2,1)}, f32[64,5120]{1,0:T(8,128)}) custom-call(s32[1,128]{1,0:T(1,128)} %bitcast.1, f32[1,5120]{1,0:T(1,128)} %gain.1, bf16[128,5120]{1,0:T(8,128)(2,1)} %rows_hbm.1, bf16[64,5120]{1,0:T(8,128)(2,1)} %lag_ref.1, f32[64,5120]{1,0:T(8,128)} %w_ref.1, bf16[256,5120]{1,0:T(8,128)(2,1)} %loss.1, bf16[256,5120]{1,0:T(8,128)(2,1)} %acts_hbm.1), custom_call_target="tpu_custom_call" | custom-call | tf_op jit(solution)/shard_map/exchange/pallas_call | solution.py:329
  80.2 0.0 copy-start
  80.2 3.5 %copy.11 = bf16[256,5120]{1,0:T(8,128)(2,1)} copy(bf16[256,5120]{1,0:T(8,128)(2,1)} %get-tuple-element.4) | data formatting | bytes 5242880
  83.7 0.0 copy-done
  83.7 1.1 %copy.12 = f32[64,5120]{1,0:T(8,128)} copy(f32[64,5120]{1,0:T(8,128)S(1)} %copy-done) | data formatting | bytes 2621440
Async XLA Ops:
  80.2 3.5 %copy-start = (f32[64,5120]{1,0:T(8,128)S(1)}, f32[64,5120]{1,0:T(8,128)}, u32[]{:S(2)}) copy-start(f32[64,5120]{1,0:T(8,128)} %get-tuple-element.5) | copy-start | bytes 3932164

commit v3 on v2

--- a/solution.py
+++ b/solution.py
@@ -51,10 +51,10 @@
     return jnp.where((dy * 2 + dh) * 32 + d * 4 + k == o, 1.0, 0.0).astype(jnp.bfloat16)
 
 
-def exchange(pieces, cols, wire, gain, rows_hbm, lag_ref, w_ref, loss, acts_hbm, out_hbm, new_w,
-             send1, recv1, send2, arrived, rows_ref, acts, grads, out, squares, products,
+def exchange(pieces, cols, wire_hbm, gain_hbm, rows_hbm, lag_ref, w_ref, loss, acts_hbm, new_w, grads_hbm, squares, products,
+             send1, recv1, send2, middle, arrived, rows_ref, acts, grads, wire, gain,
              slots, regroup, natural, lag_own, lag_in, part, part_in, fresh, w_own,
-             s0, r0, s1, r1, s2, r2, sa, ra, local, row_sem, out_sem):
+             s0, r0, s1, r1, s2, r2, s3, r3, sa, ra, local, row_sem, out_sem):
     s, z, y, h = place()
     width = lag_ref.shape[1]
     block = width // 8
@@ -89,7 +89,11 @@
     fetch_lag = pltpu.make_async_copy(lag_ref.at[:, own], lag_own, local.at[1])
     fetch_w = pltpu.make_async_copy(w_ref.at[zrows, own], w_own, local.at[2])
     fetch_acts = pltpu.make_async_copy(acts_hbm, acts, local.at[3])
+    fetch_wire = pltpu.make_async_copy(wire_hbm, wire, local.at[5])
+    fetch_gain = pltpu.make_async_copy(gain_hbm, gain, local.at[6])
     fetch_loss = pltpu.make_async_copy(loss, grads, local.at[4])
+
+    fetch_wire.start()
 
     @pl.when(s >= 1)
     def _():
@@ -97,12 +101,14 @@
             fetch(i).start()
 
     fetch_lag.start()
+    fetch_gain.start()
     fetch_w.start()
     fetch_acts.start()
     pl.when(s == 3)(fetch_loss.start)
     squares[...] = jnp.zeros_like(squares)
     products[...] = jnp.zeros_like(products)
 
+    fetch_wire.wait()
     slots[...] = slot_matrix(wire[...], z, y, h)
 
     def arrange(i):
@@ -170,6 +176,7 @@
     regroup[...] = regroup_matrix()
     natural[...] = natural_matrix(z, y, h)
     fetch_acts.wait()
+    fetch_gain.wait()
     pl.when(s == 3)(fetch_loss.wait)
 
     def onward(i):
@@ -218,21 +225,37 @@
     three = pl.ds(0, 6 * block)
 
     def relay(i):
-        data = recv1[i].reshape(SLOTS, cols)
-        send2[i] = jnp.dot(regroup[...], data, preferred_element_type=jnp.float32).astype(jnp.bfloat16)
-
-        @pl.when(s >= 1)
-        def _():
-            for e in (4, 5, 2, 3, 6, 7, 1, 0):
-                lines = pl.ds(e * 32, 32)
-                push(send2.at[i, lines, :], arrived.at[i, lines, :], s2.at[i], r2.at[i],
-                     at((s + 3) % 4, 0, e // 2, e % 2)).start()
+        data = jnp.dot(regroup[...], recv1[i].reshape(SLOTS, cols), preferred_element_type=jnp.float32)
+        data = data.astype(jnp.bfloat16).reshape(4, 64, cols)
+        send2[i] = data
+
+        @pl.when((s == 1) | (s == 3))
+        def _():
+            for dy, dh in ((2, 0), (2, 1), (1, 0), (1, 1), (3, 0), (3, 1), (0, 1), (0, 0)):
+                lines = pl.ds(dh * 32, 32)
+                push(send2.at[i, dy, lines, :], arrived.at[i, dy, lines, :], s2.at[i], r2.at[i],
+                     at(s - 1, 0, dy, dh)).start()
+
+        @pl.when(s == 2)
+        def _():
+            middle[i, 0] = data[0]
+            for dy in (2, 1, 3):
+                push(send2.at[i, dy], middle.at[i, dy], s3.at[i], r3.at[i], at(2, 0, dy, 0)).start()
 
         @pl.when(s == 0)
         def _():
             for dy in (2, 1, 3, 0):
-                lines = pl.ds(dy * 64, 64)
-                push(send2.at[i, lines, :], arrived.at[i, lines, :], s2.at[i], r2.at[i], at(1, 0, dy, 0)).start()
+                push(send2.at[i, dy], arrived.at[i, dy], s2.at[i], r2.at[i], at(1, 0, dy, 0)).start()
+
+    def three_rows(i):
+        rows = pl.ds(1, 3)
+        return push(send2.at[i, rows], middle.at[i, rows], s3.at[i], r3.at[i], at(2, 0, 1, 0))
+
+    def forward(i):
+        three_rows(i).wait_recv()
+        for dh in (1, 0):
+            lines = pl.ds(dh * 32, 32)
+            push(middle.at[i, :, lines, :], arrived.at[i, :, lines, :], s2.at[i], r2.at[i], at(1, 0, 0, dh)).start()
 
     def squared(i):
         x = acts[:, span(i)].astype(jnp.float32)
@@ -249,10 +272,18 @@
             total = total + terms[:, c * 128:(c + 1) * 128]
         products[...] = total
 
+    def keep(i):
+        return pltpu.make_async_copy(grads.at[:, span(i)], grads_hbm.at[:, span(i)], out_sem.at[i])
+
+    def take_loss(i):
+        keep(i).start()
+        multiplied(i, grads[:, span(i)].astype(jnp.float32))
+
     def take(i):
         whole(arrived, i, s2, r2).wait_recv()
-        g = jnp.dot(natural[...], arrived[i], preferred_element_type=jnp.float32)
+        g = jnp.dot(natural[...], arrived[i].reshape(SLOTS, cols), preferred_element_type=jnp.float32)
         grads[:, span(i)] = g.astype(jnp.bfloat16)
+        keep(i).start()
         multiplied(i, g)
 
     relays = lambda i: (s == 1) | (s == 3) | ((s == 2) & ~crossing(i)) | ((s == 0) & crossing(i))
@@ -266,8 +297,9 @@
         pl.when((s == 0) & ~crossing(i) & (i + 3 < pieces))(lambda: onward(i + 3))
         pl.when(i + AHEAD < pieces)(lambda: (start_out(i + AHEAD, 0), None)[1])
         pl.when(relays(i))(lambda: relay(i))
+        pl.when((s == 2) & crossing(i))(lambda: forward(i - 1))
         squared(i)
-        pl.when(s == 3)(lambda: multiplied(i, grads[:, span(i)].astype(jnp.float32)))
+        pl.when(s == 3)(lambda: take_loss(i))
         pl.when((s < 3) & (i >= LAG))(lambda: take(i - LAG))
         return carry
 
@@ -277,30 +309,13 @@
     def _():
         lax.fori_loop(pieces - LAG, pieces, lambda i, carry: (take(i), carry)[1], 0)
 
-    def emit(b):
-        rows = pl.ds(pl.multiple_of(b * 32, 32), 32)
-        return pltpu.make_async_copy(out.at[rows, :], out_hbm.at[rows, :], out_sem.at[b])
-
-    def last(b, carry):
-        for part_of in range(2):
-            rows = pl.ds(pl.multiple_of(b * 32 + part_of * 16, 16), 16)
-            r = lax.rsqrt(jnp.sum(squares[rows, :], axis=1, keepdims=True) / width + 1e-05)
-            inner = jnp.sum(products[rows, :], axis=1, keepdims=True) * r / width
-            for c in range(pieces):
-                at_cols = slice(c * cols, (c + 1) * cols)
-                x = acts[rows, at_cols].astype(jnp.float32)
-                g = grads[rows, at_cols].astype(jnp.float32)
-                out[rows, at_cols] = (g + (g * gain[:, at_cols] - (x * r) * inner) * r).astype(jnp.bfloat16)
-        emit(b).start()
-        return carry
-
-    lax.fori_loop(0, SLOTS // 32, last, 0)
-
     def finish(i, carry):
         @pl.when(relays(i))
         def _():
             along_z_all(i).wait_send()
             whole(send2, i, s2, r2).wait_send()
+
+        pl.when((s == 2) & ~crossing(i))(lambda: three_rows(i).wait_send())
 
         @pl.when((s == 2) & crossing(i))
         def _():
@@ -314,7 +329,62 @@
     push(part_in, part_in, sa.at[2], ra.at[2], me).wait_send()
     push(part, part, sa.at[3], ra.at[3], me).wait_send()
     push(new_w.at[:, three], new_w.at[:, three], sa.at[4], ra.at[4], me).wait()
-    lax.fori_loop(0, SLOTS // 32, lambda b, carry: (emit(b).wait(), carry)[1], 0)
+    lax.fori_loop(0, pieces, lambda i, carry: (keep(i).wait(), carry)[1], 0)
+
+
+def norm(cols, gain_hbm, acts_hbm, grads_hbm, squares_hbm, products_hbm, fresh, out_hbm, new_w,
+         gain, acts, grads, squares, products, out, held, small, acts_sem, grads_sem, out_sem):
+    width = acts.shape[1]
+    blocks = SLOTS // 32
+
+    def lines(b):
+        return pl.ds(pl.multiple_of(b * 32, 32), 32)
+
+    def fetch_acts(b):
+        return pltpu.make_async_copy(acts_hbm.at[lines(b), :], acts.at[lines(b), :], acts_sem.at[b])
+
+    def fetch_grads(b):
+        return pltpu.make_async_copy(grads_hbm.at[lines(b), :], grads.at[lines(b), :], grads_sem.at[b])
+
+    def emit(b):
+        return pltpu.make_async_copy(out.at[lines(b), :], out_hbm.at[lines(b), :], out_sem.at[b])
+
+    firsts = [
+        pltpu.make_async_copy(src, dst, small.at[n])
+        for n, (src, dst) in enumerate(((gain_hbm, gain), (squares_hbm, squares), (products_hbm, products)))
+    ]
+    fetch_w = pltpu.make_async_copy(fresh, held, small.at[3])
+    pass_on = pltpu.make_async_copy(held, new_w, small.at[4])
+    for copy in firsts:
+        copy.start()
+    for b in range(blocks):
+        fetch_acts(b).start()
+        fetch_grads(b).start()
+    fetch_w.start()
+    for copy in firsts:
+        copy.wait()
+
+    def last(b, carry):
+        fetch_acts(b).wait()
+        fetch_grads(b).wait()
+        for half in range(2):
+            rows = pl.ds(pl.multiple_of(b * 32 + half * 16, 16), 16)
+            r = lax.rsqrt(jnp.sum(squares[rows, :], axis=1, keepdims=True) / width + 1e-05)
+            inner = jnp.sum(products[rows, :], axis=1, keepdims=True) * r / width
+            for c in range(0, width, cols):
+                at_cols = slice(c, c + cols)
+                x = acts[rows, at_cols].astype(jnp.float32)
+                g = grads[rows, at_cols].astype(jnp.float32)
+                out[rows, at_cols] = (g + (g * gain[:, at_cols] - (x * r) * inner) * r).astype(jnp.bfloat16)
+        emit(b).start()
+        return carry
+
+    lax.fori_loop(0, blocks // 2, last, 0)
+    fetch_w.wait()
+    pass_on.start()
+    lax.fori_loop(blocks // 2, blocks, last, 0)
+    lax.fori_loop(0, blocks, lambda b, carry: (emit(b).wait(), carry)[1], 0)
+    pass_on.wait()
 
 
 def per_device(send_grads, wiring, loss_grad, saved_acts, gain, lagged_grads, weights):
@@ -326,25 +396,27 @@
     hbm = pl.BlockSpec(memory_space=pl.ANY)
     bf16, f32 = jnp.bfloat16, jnp.float32
     dma = pltpu.SemaphoreType.DMA
-    return pl.pallas_call(
+    fresh, grads, squares, products = pl.pallas_call(
         functools.partial(exchange, pieces, cols),
         out_shape=(
+            jax.ShapeDtypeStruct((depth, width), f32),
             jax.ShapeDtypeStruct((SLOTS, width), bf16),
-            jax.ShapeDtypeStruct((depth, width), f32),
+            jax.ShapeDtypeStruct((SLOTS, 128), f32),
+            jax.ShapeDtypeStruct((SLOTS, 128), f32),
         ),
-        in_specs=[vmem] * 2 + [hbm] * 5,
-        out_specs=(hbm, hbm),
+        in_specs=[hbm] * 7,
+        out_specs=(hbm, hbm, vmem, vmem),
         scratch_shapes=[
             pltpu.VMEM((pieces, 2, 128, cols), bf16),
             pltpu.VMEM((pieces, 2, 128, cols), bf16),
-            pltpu.VMEM((pieces, SLOTS, cols), bf16),
-            pltpu.VMEM((pieces, SLOTS, cols), bf16),
+            pltpu.VMEM((pieces, 4, 64, cols), bf16),
+            pltpu.VMEM((pieces, 4, 64, cols), bf16),
+            pltpu.VMEM((pieces, 4, 64, cols), bf16),
             pltpu.VMEM((rows, width), bf16),
             pltpu.VMEM((SLOTS, width), bf16),
             pltpu.VMEM((SLOTS, width), bf16),
-            pltpu.VMEM((SLOTS, width), bf16),
-            pltpu.VMEM((SLOTS, 128), f32),
-            pltpu.VMEM((SLOTS, 128), f32),
+            pltpu.VMEM((1, rows), jnp.int32),
+            pltpu.VMEM((1, width), f32),
             pltpu.VMEM((SLOTS, rows), bf16),
             pltpu.VMEM((SLOTS, SLOTS), bf16),
             pltpu.VMEM((SLOTS, SLOTS), bf16),
@@ -355,13 +427,34 @@
             pltpu.VMEM((8, block), f32),
             pltpu.VMEM((8, block), f32),
             dma((pieces,)), dma((pieces,)), dma((pieces,)), dma((pieces,)), dma((pieces,)), dma((pieces,)),
-            dma((5,)), dma((5,)), dma((5,)), dma((pieces,)), dma((SLOTS // 32,)),
+            dma((pieces,)), dma((pieces,)), dma((5,)), dma((5,)), dma((7,)), dma((pieces,)), dma((pieces,)),
         ],
         compiler_params=pltpu.CompilerParams(
-            collective_id=0, has_side_effects=True, vmem_limit_bytes=60 * 1024 * 1024
+            collective_id=0, has_side_effects=True, vmem_limit_bytes=59 * 1024 * 1024
         ),
         name="exchange",
     )(wiring.reshape(1, rows), gain, send_grads, lagged_grads, weights, loss_grad, saved_acts)
+    return pl.pallas_call(
+        functools.partial(norm, 512),
+        out_shape=(
+            jax.ShapeDtypeStruct((SLOTS, width), bf16),
+            jax.ShapeDtypeStruct((depth, width), f32),
+        ),
+        in_specs=[hbm] * 6,
+        out_specs=(hbm, hbm),
+        scratch_shapes=[
+            pltpu.VMEM((1, width), f32),
+            pltpu.VMEM((SLOTS, width), bf16),
+            pltpu.VMEM((SLOTS, width), bf16),
+            pltpu.VMEM((SLOTS, 128), f32),
+            pltpu.VMEM((SLOTS, 128), f32),
+            pltpu.VMEM((SLOTS, width), bf16),
+            pltpu.VMEM((depth, width), f32),
+            dma((5,)), dma((SLOTS // 32,)), dma((SLOTS // 32,)), dma((SLOTS // 32,)),
+        ],
+        compiler_params=pltpu.CompilerParams(vmem_limit_bytes=59 * 1024 * 1024),
+        name="norm",
+    )(gain, saved_acts, grads, squares, products, fresh)
 
 
 def solution(mesh):

time: 84.9 us -> 82.1 us (0.967)
  local copies, waits for them, and re-layouts: 4.56 us -> 0 us
  Pallas kernels: 79.5 us -> 81.4 us
    pallas_call x0 -> x1, Pallas kernels: none -> 5.04 us  [per_device(): pl.pallas_call(functools.partial(norm, 512), out_shape=(jax.ShapeDtypeStr...]
    unnamed x4 -> x0, local copies, waits for them, and re-layouts: 4.56 us -> none
    pallas_call x1, Pallas kernels: 79.5 us -> 76.4 us  [per_device(): pl.pallas_call(functools.partial(exchange, pieces, cols), out_shape=(jax....]
where the time goes in v3:
time: 82.1 us; the launch traced here: 82 us
  Pallas kernels  81.4 us (99%)
    pallas_call x1, Pallas kernels, per_device(): pl.pallas_call(functools.partial(exchange, pieces, cols), out_shape=(jax....  76.4 us
    pallas_call x1, Pallas kernels, per_device(): pl.pallas_call(functools.partial(norm, 512), out_shape=(jax.ShapeDtypeStr...  5.04 us

profile of v3, /device:TPU:1, one launch (start us, length us, event | category | flops | bytes accessed | tf_op | source)
XLA Modules:
  0.0 82.0 jit_solution(17355637821844916632)
XLA Ops:
  0.6 76.4 %exchange.1 = (f32[64,5120]{1,0:T(8,128)}, bf16[256,5120]{1,0:T(8,128)(2,1)}, f32[256,128]{1,0:T(8,128)}, f32[256,128]{1,0:T(8,128)}) custom-call(s32[1,128]{1,0:T(1,128)} %bitcast.1, f32[1,5120]{1,0:T(1,128)} %gain_hbm.3, bf16[128,5120]{1,0:T(8,128)(2,1)} %rows_hbm.1, bf16[64,5120]{1,0:T(8,128)(2,1)} %lag_ref.1, f32[64,5120]{1,0:T(8,128)} %w_ref.1, ...), custom_call_target="tpu_custom_call" | custom-call | tf_op jit(solution)/shard_map/exchange/pallas_call | solution.py:399
  77.0 5.0 %norm.1 = (bf16[256,5120]{1,0:T(8,128)(2,1)}, f32[64,5120]{1,0:T(8,128)}) custom-call(f32[1,5120]{1,0:T(1,128)} %gain_hbm.3, bf16[256,5120]{1,0:T(8,128)(2,1)} %acts_hbm.3, bf16[256,5120]{1,0:T(8,128)(2,1)} %get-tuple-element.6.grads_hbm, f32[256,128]{1,0:T(8,128)} %get-tuple-element.7.squares_hbm, f32[256,128]{1,0:T(8,128)} %get-tuple-element.8.products_hbm, ...), custom_call_target="tpu_custom_call" | custom-call | tf_op jit(solution)/shard_map/norm/pallas_call | solution.py:437

commit v4 on v3

--- a/solution.py
+++ b/solution.py
@@ -210,19 +210,28 @@
             push(fresh, new_w.at[zrows, own], sa.at[2], ra.at[2], at(s, d, 0, 0)).start()
         pltpu.make_async_copy(fresh, new_w.at[zrows, own], local.at[0]).start()
 
-    def gather_h():
+    half = new_w.shape[0] // 2
+    upper, lower = pl.ds(0, half), pl.ds(half, half)
+    pair = pl.ds(pl.multiple_of(y * 2 * block, 128), 2 * block)
+
+    def columns(n):
+        return new_w.at[upper, pl.ds(0, n * block)]
+
+    def gather_first():
         push(part_in, part_in, sa.at[2], ra.at[2], me).wait_recv()
         pltpu.make_async_copy(fresh, new_w.at[zrows, own], local.at[0]).wait()
-        push(new_w.at[:, own], new_w.at[:, own], sa.at[3], ra.at[3], at(s, 0, 0, 1)).start()
-
-    pair = pl.ds(pl.multiple_of(y * 2 * block, 128), 2 * block)
-
-    def gather_y():
-        push(part, part, sa.at[3], ra.at[3], me).wait_recv()
         for dy in (2, 1, 3):
-            push(new_w.at[:, pair], new_w.at[:, pair], sa.at[4], ra.at[4], at(s, 0, dy, 0)).start()
-
-    three = pl.ds(0, 6 * block)
+            push(new_w.at[lower, own], new_w.at[lower, own], sa.at[5], ra.at[5], at(s, 0, dy, 0)).start()
+        push(new_w.at[upper, own], new_w.at[upper, own], sa.at[3], ra.at[3], at(s, 0, 0, 1)).start()
+
+    def gather_second():
+        push(columns(1), columns(1), sa.at[3], ra.at[3], me).wait_recv()
+        for dy in (2, 1, 3):
+            push(new_w.at[upper, pair], new_w.at[upper, pair], sa.at[4], ra.at[4], at(s, 0, dy, 0)).start()
+        push(columns(3), columns(3), sa.at[5], ra.at[5], me).wait_recv()
+        for n in range(4):
+            there = pl.ds(pl.multiple_of((n * 2 + h) * block, 128), block)
+            push(new_w.at[lower, there], new_w.at[lower, there], sa.at[6], ra.at[6], at(s, 0, 0, 1)).start()
 
     def relay(i):
         data = jnp.dot(regroup[...], recv1[i].reshape(SLOTS, cols), preferred_element_type=jnp.float32)
@@ -291,8 +300,8 @@
     def step(i, carry):
         pl.when(i == 1)(lag_sum)
         pl.when(i == 3)(update)
-        pl.when(i == 5)(gather_h)
-        pl.when(i == 6)(gather_y)
+        pl.when(i == 5)(gather_first)
+        pl.when(i == 7)(gather_second)
         pl.when(relays(i))(lambda: along_z_all(i).wait_recv())
         pl.when((s == 0) & ~crossing(i) & (i + 3 < pieces))(lambda: onward(i + 3))
         pl.when(i + AHEAD < pieces)(lambda: (start_out(i + AHEAD, 0), None)[1])
@@ -327,8 +336,10 @@
     push(lag_in, lag_in, sa.at[0], ra.at[0], me).wait_send()
     push(part_in, part_in, sa.at[1], ra.at[1], me).wait_send()
     push(part_in, part_in, sa.at[2], ra.at[2], me).wait_send()
-    push(part, part, sa.at[3], ra.at[3], me).wait_send()
-    push(new_w.at[:, three], new_w.at[:, three], sa.at[4], ra.at[4], me).wait()
+    push(columns(1), columns(1), sa.at[3], ra.at[3], me).wait_send()
+    push(columns(3), columns(3), sa.at[5], ra.at[5], me).wait_send()
+    push(columns(6), columns(6), sa.at[4], ra.at[4], me).wait()
+    push(columns(4), columns(4), sa.at[6], ra.at[6], me).wait()
     lax.fori_loop(0, pieces, lambda i, carry: (keep(i).wait(), carry)[1], 0)
 
 
@@ -427,7 +438,7 @@
             pltpu.VMEM((8, block), f32),
             pltpu.VMEM((8, block), f32),
             dma((pieces,)), dma((pieces,)), dma((pieces,)), dma((pieces,)), dma((pieces,)), dma((pieces,)),
-            dma((pieces,)), dma((pieces,)), dma((5,)), dma((5,)), dma((7,)), dma((pieces,)), dma((pieces,)),
+            dma((pieces,)), dma((pieces,)), dma((7,)), dma((7,)), dma((7,)), dma((pieces,)), dma((pieces,)),
         ],
         compiler_params=pltpu.CompilerParams(
             collective_id=0, has_side_effects=True, vmem_limit_bytes=59 * 1024 * 1024

time: 82.1 us -> 78.1 us (0.951)
  Pallas kernels: 81.4 us -> 77.4 us
    pallas_call x1, Pallas kernels: 76.4 us -> 72.3 us  [per_device(): pl.pallas_call(functools.partial(exchange, pieces, cols), out_shape=(jax....]
where the time goes in v4:
time: 78.1 us; the launch traced here: 78 us
  Pallas kernels  77.4 us (99%)
    pallas_call x1, Pallas kernels, per_device(): pl.pallas_call(functools.partial(exchange, pieces, cols), out_shape=(jax....  72.3 us
    pallas_call x1, Pallas kernels, per_device(): pl.pallas_call(functools.partial(norm, 512), out_shape=(jax.ShapeDtypeStr...  5.04 us

profile of v4, /device:TPU:1, one launch (start us, length us, event | category | flops | bytes accessed | tf_op | source)
XLA Modules:
  0.0 78.0 jit_solution(13206346615264211334)
XLA Ops:
  0.6 72.3 %exchange.1 = (f32[64,5120]{1,0:T(8,128)}, bf16[256,5120]{1,0:T(8,128)(2,1)}, f32[256,128]{1,0:T(8,128)}, f32[256,128]{1,0:T(8,128)}) custom-call(s32[1,128]{1,0:T(1,128)} %bitcast.1, f32[1,5120]{1,0:T(1,128)} %gain_hbm.3, bf16[128,5120]{1,0:T(8,128)(2,1)} %rows_hbm.1, bf16[64,5120]{1,0:T(8,128)(2,1)} %lag_ref.1, f32[64,5120]{1,0:T(8,128)} %w_ref.1, ...), custom_call_target="tpu_custom_call" | custom-call | tf_op jit(solution)/shard_map/exchange/pallas_call | solution.py:410
  73.0 5.0 %norm.1 = (bf16[256,5120]{1,0:T(8,128)(2,1)}, f32[64,5120]{1,0:T(8,128)}) custom-call(f32[1,5120]{1,0:T(1,128)} %gain_hbm.3, bf16[256,5120]{1,0:T(8,128)(2,1)} %acts_hbm.3, bf16[256,5120]{1,0:T(8,128)(2,1)} %get-tuple-element.6.grads_hbm, f32[256,128]{1,0:T(8,128)} %get-tuple-element.7.squares_hbm, f32[256,128]{1,0:T(8,128)} %get-tuple-element.8.products_hbm, ...), custom_call_target="tpu_custom_call" | custom-call | tf_op jit(solution)/shard_map/norm/pallas_call | solution.py:448

commit v5 on v4

--- a/solution.py
+++ b/solution.py
@@ -163,13 +163,14 @@
 
         return carry
 
+    ahead = jnp.where(s == 2, AHEAD + 2, AHEAD)
     start_out(0, 0)
 
     @pl.when(s >= 1)
     def _():
         def arrange_start(i, carry):
             arrange(i)
-            pl.when(i < AHEAD)(lambda: (start_out(i, 0), None)[1])
+            pl.when(i < ahead)(lambda: (start_out(i, 0), None)[1])
             return carry
         lax.fori_loop(1, pieces, arrange_start, 0)
 
@@ -304,7 +305,7 @@
         pl.when(i == 7)(gather_second)
         pl.when(relays(i))(lambda: along_z_all(i).wait_recv())
         pl.when((s == 0) & ~crossing(i) & (i + 3 < pieces))(lambda: onward(i + 3))
-        pl.when(i + AHEAD < pieces)(lambda: (start_out(i + AHEAD, 0), None)[1])
+        pl.when(i + ahead < pieces)(lambda: (start_out(i + ahead, 0), None)[1])
         pl.when(relays(i))(lambda: relay(i))
         pl.when((s == 2) & crossing(i))(lambda: forward(i - 1))
         squared(i)

time: 78.1 us -> 78.9 us (1.010); the launches traced: 78 us -> 78 us
  no operation moved by 1% of the time
where the time goes in v5:
time: 78.9 us; the launch traced here: 78 us
  Pallas kernels  77.4 us (98%)
    pallas_call x1, Pallas kernels, per_device(): pl.pallas_call(functools.partial(exchange, pieces, cols), out_shape=(jax....  72.3 us
    pallas_call x1, Pallas kernels, per_device(): pl.pallas_call(functools.partial(norm, 512), out_shape=(jax.ShapeDtypeStr...  5.04 us

profile of v5, /device:TPU:1, one launch (start us, length us, event | category | flops | bytes accessed | tf_op | source)
XLA Modules:
  0.0 78.0 jit_solution(4020394390499521513)
XLA Ops:
  0.6 72.3 %exchange.1 = (f32[64,5120]{1,0:T(8,128)}, bf16[256,5120]{1,0:T(8,128)(2,1)}, f32[256,128]{1,0:T(8,128)}, f32[256,128]{1,0:T(8,128)}) custom-call(s32[1,128]{1,0:T(1,128)} %bitcast.1, f32[1,5120]{1,0:T(1,128)} %gain_hbm.3, bf16[128,5120]{1,0:T(8,128)(2,1)} %rows_hbm.1, bf16[64,5120]{1,0:T(8,128)(2,1)} %lag_ref.1, f32[64,5120]{1,0:T(8,128)} %w_ref.1, ...), custom_call_target="tpu_custom_call" | custom-call | tf_op jit(solution)/shard_map/exchange/pallas_call | solution.py:411
  73.0 5.0 %norm.1 = (bf16[256,5120]{1,0:T(8,128)(2,1)}, f32[64,5120]{1,0:T(8,128)}) custom-call(f32[1,5120]{1,0:T(1,128)} %gain_hbm.3, bf16[256,5120]{1,0:T(8,128)(2,1)} %acts_hbm.3, bf16[256,5120]{1,0:T(8,128)(2,1)} %get-tuple-element.6.grads_hbm, f32[256,128]{1,0:T(8,128)} %get-tuple-element.7.squares_hbm, f32[256,128]{1,0:T(8,128)} %get-tuple-element.8.products_hbm, ...), custom_call_target="tpu_custom_call" | custom-call | tf_op jit(solution)/shard_map/norm/pallas_call | solution.py:449
